TPU v7x, 256 devices: a whole 4x4x8 slice. The times are simulated.
256 devices in a mesh: row: 16 (over z, x_hi), col: 16 (over x_lo, y, core).
Axes of the slice: x: 4 (x_hi: 2, x_lo: 2; x = x_hi * 2 + x_lo), y: 4, z: 8, core: 2. Of those that a mesh axis runs over, the one named last changes fastest.
Arguments:
- amplitudes: bfloat16 [4096, 14336], P(('col', 'row')), may hold values from -6 to 6
- integrals: bfloat16 [14336, 14336], P('col', 'row'), may hold values from -0.046875 to 0.046875
Outputs:
- ladder: bfloat16 [4096, 14336], P(('col', 'row'))
All inputs are finite; a program needn't handle non-finite values.
Results may differ from a plain program's by a relative error of at most 0.001.
Values may be sent and summed in bfloat16 or wider, within the bound.
A program may use at most 128 MiB of HBM per device.

v0:
```python
import jax
import jax.numpy as jnp
from jax import lax
from jax.sharding import PartitionSpec as P


def body(amplitudes, integrals):
    pair_rows = lax.all_gather(amplitudes, "row", axis=0, tiled=True)
    every_block = lax.all_gather(integrals, "col", axis=0, tiled=True)
    product = jnp.dot(pair_rows, every_block, preferred_element_type=jnp.float32)
    ladder_tile = product.astype(jnp.bfloat16)
    return lax.all_to_all(ladder_tile, "row", split_axis=0, concat_axis=1, tiled=True)


def solution(mesh):
    return jax.shard_map(
        body,
        mesh=mesh,
        in_specs=(P(("col", "row"), None), P("col", "row")),
        out_specs=P(("col", "row"), None),
        check_vma=False,
    )
```

profile of v0, /device:TPU:1, one launch (start us, length us, event | category | flops | bytes accessed | tf_op | source)
XLA Modules:
  0.0 322.2 jit_solution(14909323805772111320)
XLA Ops:
  6.5 0.0 all-gather.3.cloned.1.call-start
  6.5 0.7 all-gather.3.cloned.1.call-update
  7.3 0.0 all-gather.5.cloned.1.call-start
  7.3 0.7 all-gather.5.cloned.1.call-update
  8.0 130.9 %all-gather.3.cloned.1.call-done = bf16[256,14336]{1,0:T(8,128)(2,1)} async-done(((bf16[16,14336]{1,0:T(8,128)(2,1)}), bf16[256,14336]{1,0:T(8,128)(2,1)}) %all-gather.3.cloned.1.call-update) | async-done | bytes 7340048 | tf_op jit(solution)/shard_map/all_gather | solution.py:8
  138.9 135.7 %all-gather.5.cloned.1.call-done = bf16[14336,896]{1,0:T(8,128)(2,1)} async-done(((bf16[896,896]{1,0:T(8,128)(2,1)}), bf16[14336,896]{1,0:T(8,128)(2,1)}) %all-gather.5.cloned.1.call-update) | async-done | bytes 25690128 | tf_op jit(solution)/shard_map/all_gather | solution.py:9
  274.6 14.5 %convolution_convert_fusion = bf16[256,896]{1,0:T(8,128)(2,1)S(1)} fusion(bf16[256,14336]{1,0:T(8,128)(2,1)} %all-gather.3.cloned.1.call-done, bf16[14336,896]{1,0:T(8,128)(2,1)} %all-gather.5.cloned.1.call-done), kind=kOutput, calls=%fused_computation | convolution fusion | flops 6576898048 | bytes 33488896 | tf_op jit(solution)/shard_map/dot_general | solution.py:10
  289.1 25.5 %all_to_all.19 = bf16[16,16,896]{2,1,0:T(8,128)(2,1)S(1)} all-to-all(bf16[16,16,896]{2,1,0:T(8,128)(2,1)S(1)} %bitcast.7), channel_id=1, replica_groups=mesh['row'=16,'col'=16] {'row'}, dimensions={0} | all-to-all | bytes 917504 | tf_op jit(solution)/shard_map/all_to_all | solution.py:12
  314.5 0.8 copy.4
Async XLA Ops:
  6.5 132.4 %all-gather.3.cloned.1.call-start = ((), (), s32[]{:S(2)}) async-start(), calls=%async_computation.1 | async-start | bytes 7798784 | tf_op jit(solution)/shard_map/all_gather | solution.py:8
  7.3 267.3 %all-gather.5.cloned.1.call-start = ((), (), s32[]{:S(2)}) async-start(), calls=%async_computation.2 | async-start | bytes 27295744 | tf_op jit(solution)/shard_map/all_gather | solution.py:9
Sparse Core Ops, SparseCore 0:
  9.9 128.9 all-gather.2
  140.8 133.7 all-gather.4
where the time goes:
time: 323 us; the launch traced here: 322 us
  waiting for transfers between devices  268 us (83%)
  blocking collectives  25.5 us (8%)
  matrix products  14.5 us (4%)
  between operations  13.4 us (4%)
    all_gather x1, waiting for transfers between devices, body(): every_block = lax.all_gather(integrals, 'col', axis=0, tiled=True)  136 us
    all_gather x1, waiting for transfers between devices, body(): pair_rows = lax.all_gather(amplitudes, 'row', axis=0, tiled=True)  131 us
    all_to_all x1, blocking collectives, body(): lax.all_to_all(ladder_tile, 'row', split_axis=0, concat_axis=1, tiled=True)  25.5 us
    dot_general x1, matrix products, body(): jnp.dot(pair_rows, every_block, preferred_element_type=jnp.float32)  14.5 us
  transfers between devices with their start and end apart: 2, of which 2 were waited for; matrix products, arithmetic and copies ran while one was open for 0% of the time, Pallas kernels for 0%

commit v1 on v0

v1 whole, which is shorter than its diff:
```python
import functools

import jax
import jax.numpy as jnp
from jax import lax
from jax.experimental import pallas as pl
from jax.experimental.pallas import tpu as pltpu
from jax.sharding import PartitionSpec as P

MESH = pl.DeviceIdType.MESH
BF16, F32 = jnp.bfloat16, jnp.float32

NX, NY, NZ = 4, 4, 8
ROWS = 16
BLOCK = 896
HALF = BLOCK // 2
LANES = 128
CHUNKS = BLOCK // LANES
WIDE = 2 * LANES
PAIR = 2 * BLOCK
DEEP = 4 * BLOCK
SLOTS = (0, 1, -1, 2, -2, 3, -3, 4)
SLOT_OF = {d: s for s, d in enumerate(SLOTS)}
SLOT_ROWS = NY * ROWS
SEMS = 86
AHEAD = 2

PASSES = {
    "a": (0, 2, 0, 3),
    "b": (2, 3, 0, 3),
    "c": (0, 3, 3, 5),
    "d": (3, 4, 0, 5),
    "e": (0, 4, 5, 7),
    "f": (4, 5, 0, 7),
    "g": (0, 5, 7, 8),
    "h": (5, 6, 0, 8),
    "i": (6, 7, 0, 8),
}

ORDER = (
    "B00", "S0", "B01", "S1", "B02", "B10", "A10", "B11", "B12", "A11", "Pa", "B20", "B21", "A20",
    "Qa", "B22", "Pb", "B30", "A21", "Pc", "Ra", "B31", "Qb", "B32", "Pd", "A30", "Qc", "B40", "Rb",
    "B41", "Qd", "A31", "Pe", "Rc", "B42", "Pf", "B50", "Qe", "A40", "Rd", "Pg", "B51", "Qf", "B52",
    "Ph", "Qg", "Re", "B60", "Rf", "B61", "Qh", "Rg", "B62", "Pi", "Rh", "Qi", "Ri",
)


def kernel(a_ref, b_ref, o_ref, amps, ints, part, first, second, final, landed, sems):
    row, col = lax.axis_index("row"), lax.axis_index("col")
    z, x = row // 2, (row % 2) * 2 + col // 8
    y, core = (col // 2) % NY, col % 2

    def at(dx=0, dy=0, dz=0, dk=0):
        xx, yy, zz, kk = (x + dx) % NX, (y + dy) % NY, (z + dz) % NZ, (core + dk) % 2
        return (zz * 2 + xx // 2, (xx % 2) * 8 + yy * 2 + kk)

    names = {}

    def sem(name):
        return names.setdefault(name, len(names))

    def put(send, recv, src, dst, to):
        pltpu.make_async_remote_copy(
            src_ref=src, dst_ref=dst, send_sem=sems.at[sem(("send", send))], recv_sem=sems.at[sem(recv)],
            device_id=to, device_id_type=MESH,
        ).start()

    def wait(name, like):
        pltpu.make_async_copy(like, like, sems.at[sem(name)]).wait()

    def place(j, dx, dk, r0, n):
        xx, kk = (x + dx) % NX, (core + dk) % 2
        rows = pl.multiple_of(((xx % 2) * 2 + kk) * BLOCK + r0, 16)
        return ints.at[j, pl.ds(rows, n), pl.ds(pl.multiple_of((xx // 2) * LANES, LANES), LANES)]

    for h in range(2):
        pltpu.make_async_copy(
            a_ref.at[:, pl.ds(pl.multiple_of(h * 4 * PAIR + y * PAIR, LANES), PAIR)],
            amps.at[pl.ds(pl.multiple_of(y * ROWS, ROWS), ROWS), pl.ds(h * PAIR, PAIR)],
            sems.at[sem("own a")],
        ).start()
    for j in range(CHUNKS):
        pltpu.make_async_copy(b_ref.at[:, pl.ds(j * LANES, LANES)], place(j, 0, 0, 0, BLOCK), sems.at[sem("own b")]).start()

    partners = [at(dx=1), at(dx=-1), at(dk=1)]
    partners += [at(dy=d) for d in range(1, NY)] + [at(dz=d) for d in range(1, NZ)]
    barrier = pltpu.get_barrier_semaphore()
    for to in partners:
        pl.semaphore_signal(barrier, inc=1, device_id=to, device_id_type=MESH)
    pl.semaphore_wait(barrier, len(partners))

    for h in range(2):
        for d in (2, 1, 3):
            yy = (y + d) % NY
            put(
                "spread",
                ("spread", h),
                a_ref.at[:, pl.ds(pl.multiple_of(h * 4 * PAIR + yy * PAIR, LANES), PAIR)],
                amps.at[pl.ds(pl.multiple_of(y * ROWS, ROWS), ROWS), pl.ds(h * PAIR, PAIR)],
                at(dy=d),
            )

    def direct(j):
        for step, (right, left) in enumerate(((0, HALF), (HALF, 0))):
            for dx, r0 in ((1, right), (-1, left)):
                put(
                    ("b", j), ("direct", j, step),
                    b_ref.at[pl.ds(r0, HALF), pl.ds(j * LANES, LANES)], place(j, 0, 0, r0, HALF), at(dx=dx),
                )
        put(("b", j), ("twin", j), b_ref.at[:, pl.ds(j * LANES, LANES)], place(j, 0, 0, 0, BLOCK), at(dk=1))

    for j in range(AHEAD):
        direct(j)

    def shard(d, h):
        return amps.at[pl.ds(SLOT_OF[d] * SLOT_ROWS, SLOT_ROWS), pl.ds(h * PAIR, PAIR)]

    def hand_on(d, h):
        if d < 3 or h == 0:
            put("ring", ("ring", d + 1, h % 2 if d < 3 else 0), shard(d, h), shard(d + 1, h), at(dz=-1))
        if d < 3 or h == 1:
            put("ring", ("ring", d + 1, h % 2 if d < 3 else 0), shard(-d, h), shard(4 if d == 3 else -(d + 1), h), at(dz=1))

    def event_s(h):
        if h == 0:
            wait("own a", amps.at[pl.ds(0, ROWS), :])
            wait("own b", b_ref)
        wait(("spread", h), amps.at[pl.ds(0, 3 * ROWS), pl.ds(0, PAIR)])
        hand_on(0, h)

    def event_a(d, h):
        wait(("ring", d, h), amps.at[pl.ds(0, SLOT_ROWS), :])
        if d < 4:
            hand_on(d, h)

    def event_b(j, step):
        two = ints.at[j, pl.ds(0, BLOCK), pl.ds(0, LANES)]
        if step == 0:
            wait(("direct", j, 0), two)
            for dx, r0 in ((1, 0), (-1, HALF)):
                put(("b", j), ("onward", j), place(j, -dx, 0, r0, HALF), place(j, -dx, 0, r0, HALF), at(dx=dx))
        elif step == 1:
            if j + AHEAD < CHUNKS:
                direct(j + AHEAD)
            wait(("direct", j, 1), two)
            for dx in (-1, 1):
                put(("b", j), ("twin", j), place(j, dx, 0, 0, BLOCK), place(j, dx, 0, 0, BLOCK), at(dk=1))
        else:
            wait(("onward", j), two)
            put(("b", j), ("twin", j), place(j, 2, 0, 0, BLOCK), place(j, 2, 0, 0, BLOCK), at(dk=1))
            wait(("twin", j), ints.at[j, :, pl.ds(0, LANES)])

    up, down, over = (y + 1) % NY, (y - 1) % NY, (y + 2) % NY
    LOW, HIGH = pl.ds(0, LANES), pl.ds(LANES, LANES)

    def event_p(p):
        j0, j1, s0, s1 = PASSES[p]
        js, ss = pl.ds(j0, j1 - j0), pl.ds(s0, s1 - s0)
        lhs = amps.at[pl.ds(s0 * SLOT_ROWS, (s1 - s0) * SLOT_ROWS), :]

        def one(j, carry):
            product = jnp.dot(lhs[...], ints[j], preferred_element_type=F32)
            part[j, ss] = product.reshape(s1 - s0, NY, ROWS, WIDE)
            return carry

        if j1 - j0 == 1:
            one(j0, 0)
        else:
            lax.fori_loop(j0, j1, one, 0)
        put(("p", p), ("far", p), part.at[js, ss, over, :, LOW], first.at[js, 0, ss], at(dy=1))
        put(("p", p), ("far", p), part.at[js, ss, over, :, HIGH], first.at[js, 1, ss], at(dy=-1))
        put(("p", p), ("near", p), part.at[js, ss, up, :, HIGH], second.at[js, 0, ss, :, HIGH], at(dy=1))
        put(("p", p), ("near", p), part.at[js, ss, down, :, LOW], second.at[js, 1, ss, :, LOW], at(dy=-1))

    def event_q(p):
        j0, j1, s0, s1 = PASSES[p]
        js, ss = pl.ds(j0, j1 - j0), pl.ds(s0, s1 - s0)
        wait(("far", p), first.at[js, :, ss])
        first[js, 0, ss] += part[js, ss, up, :, LOW]
        put(("q", p), ("near", p), first.at[js, 0, ss], second.at[js, 0, ss, :, LOW], at(dy=1))
        first[js, 1, ss] += part[js, ss, down, :, HIGH]
        put(("q", p), ("near", p), first.at[js, 1, ss], second.at[js, 1, ss, :, HIGH], at(dy=-1))

    def event_r(p):
        j0, j1, s0, s1 = PASSES[p]
        js, ss = pl.ds(j0, j1 - j0), pl.ds(s0, s1 - s0)
        wait(("near", p), second.at[js, :, ss])
        total = part[js, ss, y] + second[js, 0, ss] + second[js, 1, ss]
        final[js, ss] = total.astype(BF16)
        for s in sorted(range(s0, s1), key=lambda s: -abs(SLOTS[s])):
            if s == 0:
                landed[js, z] = final[js, 0]
            else:
                put("home", "home", final.at[js, s], landed.at[js, z], at(dz=SLOTS[s]))

    def flush():
        wait(("send", "spread"), amps.at[pl.ds(0, 6 * ROWS), pl.ds(0, PAIR)])
        wait(("send", "ring"), amps.at[pl.ds(0, 7 * SLOT_ROWS), :])
        for j in range(CHUNKS):
            wait(("send", ("b", j)), ints.at[j, pl.ds(0, 7 * HALF), :])
        for p, (j0, j1, s0, s1) in PASSES.items():
            js, ss = pl.ds(j0, j1 - j0), pl.ds(s0, s1 - s0)
            wait(("send", ("p", p)), second.at[js, :, ss])
            wait(("send", ("q", p)), first.at[js, :, ss])
        wait(("send", "home"), final.at[:, pl.ds(1, NZ - 1)])

    for event in ORDER:
        kind, rest = event[0], event[1:]
        if kind == "S":
            event_s(int(rest))
        elif kind == "A":
            event_a(int(rest[0]), int(rest[1]))
        elif kind == "B":
            event_b(int(rest[0]), int(rest[1]))
        elif kind == "P":
            event_p(rest)
        elif kind == "Q":
            event_q(rest)
        else:
            event_r(rest)

    wait("home", final.at[:, pl.ds(1, NZ - 1)])
    for zz in range(NZ):
        for j in range(CHUNKS):
            for half in range(2):
                o_ref[:, pl.ds(zz * PAIR + half * BLOCK + j * LANES, LANES)] = landed[j, zz, :, pl.ds(half * LANES, LANES)]
    flush()
    assert len(names) == SEMS, len(names)


def body(amplitudes, integrals):
    return pl.pallas_call(
        kernel,
        out_shape=jax.ShapeDtypeStruct((ROWS, NZ * PAIR), BF16),
        in_specs=[pl.BlockSpec(memory_space=pl.ANY)] * 2,
        out_specs=pl.BlockSpec(memory_space=pltpu.VMEM),
        scratch_shapes=[
            pltpu.VMEM((NZ * SLOT_ROWS, DEEP), BF16),
            pltpu.VMEM((CHUNKS, DEEP, WIDE), BF16),
            pltpu.VMEM((CHUNKS, NZ, NY, ROWS, WIDE), F32),
            pltpu.VMEM((CHUNKS, 2, NZ, ROWS, LANES), F32),
            pltpu.VMEM((CHUNKS, 2, NZ, ROWS, WIDE), F32),
            pltpu.VMEM((CHUNKS, NZ, ROWS, WIDE), BF16),
            pltpu.VMEM((CHUNKS, NZ, ROWS, WIDE), BF16),
            pltpu.SemaphoreType.DMA((SEMS,)),
        ],
        compiler_params=pltpu.CompilerParams(collective_id=0, has_side_effects=True, vmem_limit_bytes=56 << 20),
        cost_estimate=pl.CostEstimate(flops=2 * 512 * DEEP * PAIR, bytes_accessed=4 << 20, transcendentals=0),
    )(amplitudes, integrals)


def solution(mesh):
    return jax.shard_map(
        body,
        mesh=mesh,
        in_specs=(P(("col", "row"), None), P("col", "row")),
        out_specs=P(("col", "row"), None),
        check_vma=False,
    )
```

time: 323 us -> 90.2 us (0.28)
  waiting for transfers between devices: 268 us -> 0 us
  Pallas kernels: 0 us -> 88.3 us
  blocking collectives: 25.5 us -> 0 us
  matrix products: 14.5 us -> 0 us
  between operations: 13.4 us -> 0.01 us
    all_gather x2 -> x0, waiting for transfers between devices: 267 us -> none  [the longest x1 136 us: body(): every_block = lax.all_gather(integrals, 'col', axis=0, tiled=True)]
    pallas_call x0 -> x1, Pallas kernels: none -> 88.3 us  [body(): pl.pallas_call(kernel, out_shape=jax.ShapeDtypeStruct((ROWS, NZ * PAIR),...]
    all_to_all x1 -> x0, blocking collectives: 25.5 us -> none  [body(): lax.all_to_all(ladder_tile, 'row', split_axis=0, concat_axis=1, tiled=True)]
    dot_general x1 -> x0, matrix products: 14.5 us -> none  [body(): jnp.dot(pair_rows, every_block, preferred_element_type=jnp.float32)]
  transfers between devices with their start and end apart: 2 -> 0, of which waited for: 2 -> 0; matrix products, arithmetic and copies ran while one was open for 0% -> 0% of each run, Pallas kernels for 0% -> 0%
where the time goes in v1:
time: 90.2 us; the launch traced here: 90.1 us
  Pallas kernels  88.3 us (98%)
  local copies, waits for them, and re-layouts  1.82 us (2%)
    pallas_call x1, Pallas kernels, body(): pl.pallas_call(kernel, out_shape=jax.ShapeDtypeStruct((ROWS, NZ * PAIR),...  88.3 us
    unnamed x1, local copies, waits for them, and re-layouts  1.82 us

profile of v1, /device:TPU:1, one launch (start us, length us, event | category | flops | bytes accessed | tf_op | source)
XLA Modules:
  0.0 90.1 jit_solution(1872986314982679320)
XLA Ops:
  0.0 88.3 %shard_map.28 = bf16[16,14336]{1,0:T(8,128)(2,1)} custom-call(bf16[16,14336]{1,0:T(8,128)(2,1)} %a_ref.1, bf16[896,896]{1,0:T(8,128)(2,1)} %b_ref.1), custom_call_target="tpu_custom_call" | custom-call | flops 6576668672 | bytes 4194304 | tf_op jit(solution)/shard_map/pallas_call | solution.py:232
  88.3 1.8 %copy.4 = bf16[16,14336]{1,0:T(8,128)(2,1)} copy(bf16[16,14336]{1,0:T(8,128)(2,1)} %shard_map.28) | data formatting | bytes 917504

commit v2 on v1

v2 whole, which is shorter than its diff:
```python
import functools

import jax
import jax.numpy as jnp
from jax import lax
from jax.experimental import pallas as pl
from jax.experimental.pallas import tpu as pltpu
from jax.sharding import PartitionSpec as P

MESH = pl.DeviceIdType.MESH
BF16, F32 = jnp.bfloat16, jnp.float32

NX, NY, NZ = 4, 4, 8
ROWS = 16
BLOCK = 896
HALF = BLOCK // 2
LANES = 128
CHUNKS = BLOCK // LANES
WIDE = 2 * LANES
PAIR = 2 * BLOCK
DEEP = 4 * BLOCK
SLOTS = (0, 1, -1, 2, -2, 3, -3, 4)
SLOT_OF = {d: s for s, d in enumerate(SLOTS)}
SLOT_ROWS = NY * ROWS
SEMS = 77
SENDS = {
    None: ((0, 0), (0, 1), (1, 0)),
    0: ((1, 1), (2, 0)),
    1: ((2, 1), (3, 0)),
    2: ((3, 1), (4, 0)),
    3: ((4, 1), (5, 0)),
    4: ((5, 1),),
    5: ((6, 0), (6, 1)),
    6: (),
}

PASSES = {
    "a": (0, 1, 0, 3),
    "b": (1, 2, 0, 3),
    "c": (0, 2, 3, 5),
    "d": (2, 3, 0, 5),
    "e": (0, 3, 5, 7),
    "f": (3, 4, 0, 7),
    "g": (0, 4, 7, 8),
    "h": (4, 5, 0, 8),
    "i": (5, 6, 0, 8),
}
LAST = CHUNKS - 1

ORDER = (
    "S1", "S3", "B00", "S2", "A10", "B01", "A11", "B10", "A13", "B02", "A12", "B03", "Pa", "B11", "A20", "B20",
    "A21", "B12", "A23", "B13", "Pb", "B21", "Qa", "A22", "B30", "Pc", "A30", "B22", "Qb", "Ra", "A31", "B23",
    "Pd", "B31", "Qc", "A33", "B40", "Rb", "A32", "Pe", "B32", "Qd", "B33", "Pf", "B41", "Rc", "A40", "Qe",
    "B50", "Pg", "B42", "Rd", "B43", "Ph", "B51", "Qf", "B52", "Qg", "B53", "Qh", "B60", "Pi", "Re", "B61",
    "Rf", "PO", "B62", "Qi", "B63", "PF", "Rg", "Rh", "RO1", "RO0", "RF1", "Ri", "RF0",
)


def kernel(a_ref, b_ref, o_ref, amps, ints, part, first, second, final, landed, rest, sems):
    row, col = lax.axis_index("row"), lax.axis_index("col")
    z, x = row // 2, (row % 2) * 2 + col // 8
    y, core = (col // 2) % NY, col % 2

    def at(dx=0, dy=0, dz=0, dk=0):
        xx, yy, zz, kk = (x + dx) % NX, (y + dy) % NY, (z + dz) % NZ, (core + dk) % 2
        return (zz * 2 + xx // 2, (xx % 2) * 8 + yy * 2 + kk)

    names = {}

    def sem(name):
        return names.setdefault(name, len(names))

    def put(send, recv, src, dst, to):
        pltpu.make_async_remote_copy(
            src_ref=src, dst_ref=dst, send_sem=sems.at[sem(("send", send))], recv_sem=sems.at[sem(recv)],
            device_id=to, device_id_type=MESH,
        ).start()

    def wait(name, like):
        pltpu.make_async_copy(like, like, sems.at[sem(name)]).wait()

    def place(j, dx, dk, r0, n):
        xx, kk = (x + dx) % NX, (core + dk) % 2
        rows = pl.multiple_of(((xx % 2) * 2 + kk) * BLOCK + r0, 16)
        return ints.at[j, pl.ds(rows, n), pl.ds(pl.multiple_of((xx // 2) * LANES, LANES), LANES)]

    for h in range(2):
        pltpu.make_async_copy(
            a_ref.at[:, pl.ds(pl.multiple_of(h * 4 * PAIR + y * PAIR, LANES), PAIR)],
            amps.at[pl.ds(pl.multiple_of(y * ROWS, ROWS), ROWS), pl.ds(h * PAIR, PAIR)],
            sems.at[sem("own a")],
        ).start()
    for j in range(CHUNKS):
        pltpu.make_async_copy(b_ref.at[:, pl.ds(j * LANES, LANES)], place(j, 0, 0, 0, BLOCK), sems.at[sem("own b")]).start()

    partners = [at(dx=1), at(dx=-1), at(dk=1)]
    partners += [at(dy=d) for d in range(1, NY)] + [at(dz=d) for d in range(1, NZ)]
    barrier = pltpu.get_barrier_semaphore()
    for to in partners:
        pl.semaphore_signal(barrier, inc=1, device_id=to, device_id_type=MESH)
    pl.semaphore_wait(barrier, len(partners))

    def rows_of(d, dy):
        return pl.ds(pl.multiple_of(SLOT_OF[d] * SLOT_ROWS + (y + dy) % NY * ROWS, ROWS), ROWS)

    def hand_on(d, q):
        if d < 3 or q < 2:
            put("ring", ("ring", d + 1, q if d < 3 else 0), amps.at[rows_of(d, q), :], amps.at[rows_of(d + 1, q), :], at(dz=-1))
        if d < 3 or q >= 2:
            put("ring", ("ring", d + 1, q if d < 3 else 0), amps.at[rows_of(-d, q), :], amps.at[rows_of(4 if d == 3 else -(d + 1), q), :], at(dz=1))

    wait("own a", amps.at[pl.ds(0, ROWS), :])
    hand_on(0, 0)

    for d in (1, 3, 2):
        yy = (y + d) % NY
        for h in range(2):
            put(
                "spread",
                ("spread", NY - d),
                a_ref.at[:, pl.ds(pl.multiple_of(h * 4 * PAIR + yy * PAIR, LANES), PAIR)],
                amps.at[rows_of(0, 0), pl.ds(h * PAIR, PAIR)],
                at(dy=d),
            )

    def direct(j, step):
        for dx, r0 in ((1, step * HALF), (-1, (1 - step) * HALF)):
            put(
                "b", ("direct", j, step),
                b_ref.at[pl.ds(r0, HALF), pl.ds(j * LANES, LANES)], place(j, 0, 0, r0, HALF), at(dx=dx),
            )
        if step == 1:
            put("b", ("twin", j), b_ref.at[:, pl.ds(j * LANES, LANES)], place(j, 0, 0, 0, BLOCK), at(dk=1))

    for half in SENDS[None]:
        direct(*half)

    def event_s(q):
        wait(("spread", q), amps.at[pl.ds(0, ROWS), :])
        hand_on(0, q)

    def event_a(d, q):
        wait(("ring", d, q), amps.at[pl.ds(0, (4 if d == 4 else 2) * ROWS), :])
        if d < 4:
            hand_on(d, q)

    def event_b(j, step):
        two = ints.at[j, pl.ds(0, BLOCK), pl.ds(0, LANES)]
        if step == 0:
            wait(("direct", j, 0), two)
            for dx, r0 in ((1, 0), (-1, HALF)):
                put("b", ("onward", j), place(j, -dx, 0, r0, HALF), place(j, -dx, 0, r0, HALF), at(dx=dx))
            for half in SENDS[j]:
                direct(*half)
        elif step == 3:
            if j == 0:
                wait("own b", b_ref)
            if j == LAST:
                wait(("twin", j, "last"), two)
            else:
                wait(("twin", j), ints.at[j, :, pl.ds(0, LANES)])
        elif step == 1:
            wait(("direct", j, 1), two)
            for dx in (-1, 1):
                put("b", ("twin", j), place(j, dx, 0, 0, BLOCK), place(j, dx, 0, 0, BLOCK), at(dk=1))
        else:
            wait(("onward", j), two)
            name = ("twin", j, "last") if j == LAST else ("twin", j)
            put("b", name, place(j, 2, 0, 0, BLOCK), place(j, 2, 0, 0, BLOCK), at(dk=1))

    up, down, over = (y + 1) % NY, (y - 1) % NY, (y + 2) % NY
    LOW, HIGH = pl.ds(0, LANES), pl.ds(LANES, LANES)

    def event_p(p):
        j0, j1, s0, s1 = PASSES[p]
        js, ss = pl.ds(j0, j1 - j0), pl.ds(s0, s1 - s0)

        def one(j, carry):
            for m0, m1 in ((s0, s1),) if s1 - s0 < NZ else ((0, NZ // 2), (NZ // 2, NZ)):
                product = jnp.dot(amps[pl.ds(m0 * SLOT_ROWS, (m1 - m0) * SLOT_ROWS)], ints[j], preferred_element_type=F32)
                part[j, pl.ds(m0, m1 - m0)] = product.reshape(m1 - m0, NY, ROWS, WIDE)
            return carry

        if j1 - j0 == 1:
            one(j0, 0)
        else:
            lax.fori_loop(j0, j1, one, 0)
        put("p", ("far", p), part.at[js, ss, over, :, LOW], first.at[js, 0, ss], at(dy=1))
        put("p", ("far", p), part.at[js, ss, over, :, HIGH], first.at[js, 1, ss], at(dy=-1))
        put("p", ("near", p), part.at[js, ss, up, :, HIGH], second.at[js, 0, ss, :, HIGH], at(dy=1))
        put("p", ("near", p), part.at[js, ss, down, :, LOW], second.at[js, 1, ss, :, LOW], at(dy=-1))

    def event_q(p):
        j0, j1, s0, s1 = PASSES[p]
        js, ss = pl.ds(j0, j1 - j0), pl.ds(s0, s1 - s0)
        wait(("far", p), first.at[js, :, ss])
        first[js, 0, ss] += part[js, ss, up, :, LOW]
        put("q", ("near", p), first.at[js, 0, ss], second.at[js, 0, ss, :, LOW], at(dy=1))
        first[js, 1, ss] += part[js, ss, down, :, HIGH]
        put("q", ("near", p), first.at[js, 1, ss], second.at[js, 1, ss, :, HIGH], at(dy=-1))

    def event_r(p):
        j0, j1, s0, s1 = PASSES[p]
        js, ss = pl.ds(j0, j1 - j0), pl.ds(s0, s1 - s0)
        wait(("near", p), second.at[js, :, ss])
        total = part[js, ss, y] + second[js, 0, ss] + second[js, 1, ss]
        final[js, ss] = total.astype(BF16)
        for s in sorted(range(s0, s1), key=lambda s: -abs(SLOTS[s])):
            if s == 0:
                landed[js, z] = final[js, 0]
            else:
                put("home", "home", final.at[js, s], landed.at[js, z], at(dz=SLOTS[s]))

    def lane(own):
        return pl.ds(pl.multiple_of((x // 2 if own else 1 - x // 2) * LANES, LANES), LANES)

    def deep(near):
        return pl.ds(pl.multiple_of((1 - x % 2 if near else x % 2) * PAIR, LANES), PAIR)

    def share(ss, k, lanes, width):
        rows = pl.ds(ss.start * SLOT_ROWS, ss.size * SLOT_ROWS)
        product = jnp.dot(amps[rows, k], ints[LAST, k, lanes], preferred_element_type=F32)
        return product.reshape(ss.size, NY, ROWS, width)

    halves = (pl.ds(0, NZ // 2), pl.ds(NZ // 2, NZ // 2))

    def last_p(own, k):
        here = lane(own)
        for half in (1, 0):
            ss = halves[half]
            part[LAST, ss, :, :, here] += share(ss, k, here, LANES)
            for d in (2, 1, 3):
                put("rest", ("rest", own, half), part.at[LAST, ss, (y + d) % NY, :, here], rest.at[int(own), d - 1, ss], at(dy=d))

    def last_r(own, half):
        here, ss, o = lane(own), halves[half], int(own)
        wait(("rest", own, half), rest.at[o, :, ss])
        total = part[LAST, ss, y, :, here] + rest[o, 0, ss] + rest[o, 1, ss] + rest[o, 2, ss]
        final[LAST, ss, :, here] = total.astype(BF16)
        for s in range(ss.start + ss.size - 1, max(ss.start, 1) - 1, -1):
            put("home", "home", final.at[LAST, s, :, here], landed.at[LAST, z, :, here], at(dz=SLOTS[s]))
        if half == 0:
            landed[LAST, z, :, here] = final[LAST, 0, :, here]

    def own_p():
        wait(("twin", LAST), ints.at[LAST, pl.ds(0, 3 * BLOCK), pl.ds(0, LANES)])
        for ss in halves:
            part[LAST, ss] = share(ss, deep(True), pl.ds(0, WIDE), WIDE)
        last_p(True, deep(False))

    def flush():
        wait(("send", "spread"), amps.at[pl.ds(0, 6 * ROWS), pl.ds(0, PAIR)])
        wait(("send", "ring"), amps.at[pl.ds(0, 7 * SLOT_ROWS), :])
        wait(("send", "b"), ints.at[:, pl.ds(0, 7 * HALF), :])
        wait(("send", "p"), second)
        wait(("send", "q"), first)
        wait(("send", "rest"), rest)
        wait(("send", "home"), final.at[:, pl.ds(1, NZ - 1)])

    ends = {"PO": own_p, "PF": functools.partial(last_p, False, deep(False))}
    ends |= {f"R{c}{half}": functools.partial(last_r, c == "O", half) for c in "OF" for half in range(2)}
    for event in ORDER:
        kind, which = event[0], event[1:]
        if kind == "S":
            event_s(int(which))
        elif kind == "A":
            event_a(int(which[0]), int(which[1]))
        elif kind == "B":
            event_b(int(which[0]), int(which[1]))
        elif event in ends:
            ends[event]()
        elif kind == "P":
            event_p(which)
        elif kind == "Q":
            event_q(which)
        else:
            event_r(which)

    wait("home", final.at[:, pl.ds(1, NZ - 1)])
    for zz in range(NZ):
        for j in range(CHUNKS):
            for half in range(2):
                o_ref[:, pl.ds(zz * PAIR + half * BLOCK + j * LANES, LANES)] = landed[j, zz, :, pl.ds(half * LANES, LANES)]
    flush()
    assert len(names) == SEMS, len(names)


def body(amplitudes, integrals):
    return pl.pallas_call(
        kernel,
        out_shape=jax.ShapeDtypeStruct((ROWS, NZ * PAIR), BF16),
        in_specs=[pl.BlockSpec(memory_space=pl.ANY)] * 2,
        out_specs=pl.BlockSpec(memory_space=pltpu.VMEM),
        scratch_shapes=[
            pltpu.VMEM((NZ * SLOT_ROWS, DEEP), BF16),
            pltpu.VMEM((CHUNKS, DEEP, WIDE), BF16),
            pltpu.VMEM((CHUNKS, NZ, NY, ROWS, WIDE), F32),
            pltpu.VMEM((LAST, 2, NZ, ROWS, LANES), F32),
            pltpu.VMEM((LAST, 2, NZ, ROWS, WIDE), F32),
            pltpu.VMEM((CHUNKS, NZ, ROWS, WIDE), BF16),
            pltpu.VMEM((CHUNKS, NZ, ROWS, WIDE), BF16),
            pltpu.VMEM((2, NY - 1, NZ, ROWS, LANES), F32),
            pltpu.SemaphoreType.DMA((SEMS,)),
        ],
        compiler_params=pltpu.CompilerParams(collective_id=0, has_side_effects=True, vmem_limit_bytes=56 << 20),
        cost_estimate=pl.CostEstimate(flops=2 * 512 * DEEP * PAIR, bytes_accessed=4 << 20, transcendentals=0),
    )(amplitudes, integrals)


def solution(mesh):
    return jax.shard_map(
        body,
        mesh=mesh,
        in_specs=(P(("col", "row"), None), P("col", "row")),
        out_specs=P(("col", "row"), None),
        check_vma=False,
    )
```

time: 90.2 us -> 80.2 us (0.89)
  Pallas kernels: 88.3 us -> 78.2 us
    pallas_call x1, Pallas kernels: 88.3 us -> 78.2 us  [body(): pl.pallas_call(kernel, out_shape=jax.ShapeDtypeStruct((ROWS, NZ * PAIR),...]
where the time goes in v2:
time: 80.2 us; the launch traced here: 80.1 us
  Pallas kernels  78.2 us (98%)
  local copies, waits for them, and re-layouts  1.82 us (2%)
    pallas_call x1, Pallas kernels, body(): pl.pallas_call(kernel, out_shape=jax.ShapeDtypeStruct((ROWS, NZ * PAIR),...  78.2 us
    unnamed x1, local copies, waits for them, and re-layouts  1.82 us

profile of v2, /device:TPU:1, one launch (start us, length us, event | category | flops | bytes accessed | tf_op | source)
XLA Modules:
  0.0 80.1 jit_solution(17987301350765340529)
XLA Ops:
  0.0 78.2 %shard_map.28 = bf16[16,14336]{1,0:T(8,128)(2,1)} custom-call(bf16[16,14336]{1,0:T(8,128)(2,1)} %a_ref.1, bf16[896,896]{1,0:T(8,128)(2,1)} %b_ref.1), custom_call_target="tpu_custom_call" | custom-call | flops 6576668672 | bytes 4194304 | tf_op jit(solution)/shard_map/pallas_call | solution.py:289
  78.2 1.8 %copy.4 = bf16[16,14336]{1,0:T(8,128)(2,1)} copy(bf16[16,14336]{1,0:T(8,128)(2,1)} %shard_map.28) | data formatting | bytes 917504

commit v3 on v2

--- a/solution.py
+++ b/solution.py
@@ -22,7 +22,7 @@
 SLOTS = (0, 1, -1, 2, -2, 3, -3, 4)
 SLOT_OF = {d: s for s, d in enumerate(SLOTS)}
 SLOT_ROWS = NY * ROWS
-SEMS = 77
+SEMS = 83
 SENDS = {
     None: ((0, 0), (0, 1), (1, 0)),
     0: ((1, 1), (2, 0)),
@@ -42,17 +42,17 @@
     "e": (0, 3, 5, 7),
     "f": (3, 4, 0, 7),
     "g": (0, 4, 7, 8),
-    "h": (4, 5, 0, 8),
-    "i": (5, 6, 0, 8),
 }
 LAST = CHUNKS - 1
+SPLIT = (4, 5, LAST)
 
 ORDER = (
     "S1", "S3", "B00", "S2", "A10", "B01", "A11", "B10", "A13", "B02", "A12", "B03", "Pa", "B11", "A20", "B20",
     "A21", "B12", "A23", "B13", "Pb", "B21", "Qa", "A22", "B30", "Pc", "A30", "B22", "Qb", "Ra", "A31", "B23",
-    "Pd", "B31", "Qc", "A33", "B40", "Rb", "A32", "Pe", "B32", "Qd", "B33", "Pf", "B41", "Rc", "A40", "Qe",
-    "B50", "Pg", "B42", "Rd", "B43", "Ph", "B51", "Qf", "B52", "Qg", "B53", "Qh", "B60", "Pi", "Re", "B61",
-    "Rf", "PO", "B62", "Qi", "B63", "PF", "Rg", "Rh", "RO1", "RO0", "RF1", "Ri", "RF0",
+    "Pd", "B31", "Qc", "A33", "B40", "Rb", "A32", "Pe", "B32", "Qd", "B33", "Pf", "B41", "A40", "Qe", "B50",
+    "O4P", "Rc", "Pg", "B42", "Rd", "B43", "F4P", "B51", "Qf", "O4Q", "B52", "Qg", "O5P", "B60", "B53", "F5P",
+    "F4Q", "B61", "Re", "O5Q", "O6P", "B62", "O4R", "F5Q", "B63", "F6P", "Rf", "Rg", "F4R", "O5R", "O6R", "O6S",
+    "F5R", "F6R", "F6S",
 )
 
 
@@ -94,7 +94,7 @@
         pltpu.make_async_copy(b_ref.at[:, pl.ds(j * LANES, LANES)], place(j, 0, 0, 0, BLOCK), sems.at[sem("own b")]).start()
 
     partners = [at(dx=1), at(dx=-1), at(dk=1)]
-    partners += [at(dy=d) for d in range(1, NY)] + [at(dz=d) for d in range(1, NZ)]
+    partners += [at(dy=d) for d in range(1, NY)] + [at(dz=1), at(dz=-1)]
     barrier = pltpu.get_barrier_semaphore()
     for to in partners:
         pl.semaphore_signal(barrier, inc=1, device_id=to, device_id_type=MESH)
@@ -155,7 +155,7 @@
         elif step == 3:
             if j == 0:
                 wait("own b", b_ref)
-            if j == LAST:
+            if j in SPLIT:
                 wait(("twin", j, "last"), two)
             else:
                 wait(("twin", j), ints.at[j, :, pl.ds(0, LANES)])
@@ -165,7 +165,7 @@
                 put("b", ("twin", j), place(j, dx, 0, 0, BLOCK), place(j, dx, 0, 0, BLOCK), at(dk=1))
         else:
             wait(("onward", j), two)
-            name = ("twin", j, "last") if j == LAST else ("twin", j)
+            name = ("twin", j, "last") if j in SPLIT else ("twin", j)
             put("b", name, place(j, 2, 0, 0, BLOCK), place(j, 2, 0, 0, BLOCK), at(dk=1))
 
     up, down, over = (y + 1) % NY, (y - 1) % NY, (y + 2) % NY
@@ -176,7 +176,7 @@
         js, ss = pl.ds(j0, j1 - j0), pl.ds(s0, s1 - s0)
 
         def one(j, carry):
-            for m0, m1 in ((s0, s1),) if s1 - s0 < NZ else ((0, NZ // 2), (NZ // 2, NZ)):
+            for m0, m1 in ((s0, s1),) if s1 - s0 < 6 else ((s0, NZ // 2), (NZ // 2, s1)):
                 product = jnp.dot(amps[pl.ds(m0 * SLOT_ROWS, (m1 - m0) * SLOT_ROWS)], ints[j], preferred_element_type=F32)
                 part[j, pl.ds(m0, m1 - m0)] = product.reshape(m1 - m0, NY, ROWS, WIDE)
             return carry
@@ -217,36 +217,67 @@
     def deep(near):
         return pl.ds(pl.multiple_of((1 - x % 2 if near else x % 2) * PAIR, LANES), PAIR)
 
-    def share(ss, k, lanes, width):
+    def share(j, ss, k, lanes, width):
         rows = pl.ds(ss.start * SLOT_ROWS, ss.size * SLOT_ROWS)
-        product = jnp.dot(amps[rows, k], ints[LAST, k, lanes], preferred_element_type=F32)
+        product = jnp.dot(amps[rows, k], ints[j, k, lanes], preferred_element_type=F32)
         return product.reshape(ss.size, NY, ROWS, width)
 
     halves = (pl.ds(0, NZ // 2), pl.ds(NZ // 2, NZ // 2))
 
-    def last_p(own, k):
+    def own_products(j):
+        wait(("twin", j), ints.at[j, pl.ds(0, 3 * BLOCK), pl.ds(0, LANES)])
+        for ss in halves:
+            part[j, ss] = share(j, ss, deep(True), pl.ds(0, WIDE), WIDE)
+
+    def split_p(j, own):
+        u, d = halves if own else halves[::-1]
         here = lane(own)
+        if own:
+            own_products(j)
+        for ss in halves:
+            part[j, ss, :, :, here] += share(j, ss, deep(False), here, LANES)
+        put("p", ("far", j, own), part.at[j, u, over, :, here], first.at[j, 0, u], at(dy=1))
+        put("p", ("far", j, own), part.at[j, d, over, :, here], first.at[j, 1, d], at(dy=-1))
+        put("p", ("near", j, own), part.at[j, d, up, :, here], second.at[j, 0, d, :, here], at(dy=1))
+        put("p", ("near", j, own), part.at[j, u, down, :, here], second.at[j, 1, u, :, here], at(dy=-1))
+
+    def split_q(j, own):
+        u, d = halves if own else halves[::-1]
+        here = lane(own)
+        wait(("far", j, own), first.at[j, 0])
+        first[j, 0, u] += part[j, u, up, :, here]
+        put("q", ("near", j, own), first.at[j, 0, u], second.at[j, 0, u, :, here], at(dy=1))
+        first[j, 1, d] += part[j, d, down, :, here]
+        put("q", ("near", j, own), first.at[j, 1, d], second.at[j, 1, d, :, here], at(dy=-1))
+
+    def settle(j, ss, here, total):
+        final[j, ss, :, here] = total.astype(BF16)
+        for s in range(ss.start + ss.size - 1, max(ss.start, 1) - 1, -1):
+            put("home", "home", final.at[j, s, :, here], landed.at[j, z, :, here], at(dz=SLOTS[s]))
+        if ss.start == 0:
+            landed[j, z, :, here] = final[j, 0, :, here]
+
+    def split_r(j, own):
+        here = lane(own)
+        wait(("near", j, own), second.at[j, 0])
+        settle(j, pl.ds(0, NZ), here, part[j, :, y, :, here] + second[j, 0, :, :, here] + second[j, 1, :, :, here])
+
+    def last_p(own):
+        here = lane(own)
+        if own:
+            own_products(LAST)
         for half in (1, 0):
             ss = halves[half]
-            part[LAST, ss, :, :, here] += share(ss, k, here, LANES)
+            part[LAST, ss, :, :, here] += share(LAST, ss, deep(False), here, LANES)
             for d in (2, 1, 3):
                 put("rest", ("rest", own, half), part.at[LAST, ss, (y + d) % NY, :, here], rest.at[int(own), d - 1, ss], at(dy=d))
 
     def last_r(own, half):
         here, ss, o = lane(own), halves[half], int(own)
         wait(("rest", own, half), rest.at[o, :, ss])
-        total = part[LAST, ss, y, :, here] + rest[o, 0, ss] + rest[o, 1, ss] + rest[o, 2, ss]
-        final[LAST, ss, :, here] = total.astype(BF16)
-        for s in range(ss.start + ss.size - 1, max(ss.start, 1) - 1, -1):
-            put("home", "home", final.at[LAST, s, :, here], landed.at[LAST, z, :, here], at(dz=SLOTS[s]))
-        if half == 0:
-            landed[LAST, z, :, here] = final[LAST, 0, :, here]
-
-    def own_p():
-        wait(("twin", LAST), ints.at[LAST, pl.ds(0, 3 * BLOCK), pl.ds(0, LANES)])
-        for ss in halves:
-            part[LAST, ss] = share(ss, deep(True), pl.ds(0, WIDE), WIDE)
-        last_p(True, deep(False))
+        settle(LAST, ss, here, part[LAST, ss, y, :, here] + rest[o, 0, ss] + rest[o, 1, ss] + rest[o, 2, ss])
+
+    homes = final.at[:, pl.ds(1, NZ - 1)]
 
     def flush():
         wait(("send", "spread"), amps.at[pl.ds(0, 6 * ROWS), pl.ds(0, PAIR)])
@@ -255,20 +286,26 @@
         wait(("send", "p"), second)
         wait(("send", "q"), first)
         wait(("send", "rest"), rest)
-        wait(("send", "home"), final.at[:, pl.ds(1, NZ - 1)])
-
-    ends = {"PO": own_p, "PF": functools.partial(last_p, False, deep(False))}
-    ends |= {f"R{c}{half}": functools.partial(last_r, c == "O", half) for c in "OF" for half in range(2)}
+        wait(("send", "home"), homes)
+
+    ends = {}
+    for part_of, own in (("O", True), ("F", False)):
+        ends[f"{part_of}6P"] = functools.partial(last_p, own)
+        ends[f"{part_of}6R"] = functools.partial(last_r, own, 1)
+        ends[f"{part_of}6S"] = functools.partial(last_r, own, 0)
+    for step, do in (("P", split_p), ("Q", split_q), ("R", split_r)):
+        ends |= {f"O{j}{step}": functools.partial(do, j, True) for j in SPLIT[:-1]}
+        ends |= {f"F{j}{step}": functools.partial(do, j, False) for j in SPLIT[:-1]}
     for event in ORDER:
         kind, which = event[0], event[1:]
-        if kind == "S":
+        if event in ends:
+            ends[event]()
+        elif kind == "S":
             event_s(int(which))
         elif kind == "A":
             event_a(int(which[0]), int(which[1]))
         elif kind == "B":
             event_b(int(which[0]), int(which[1]))
-        elif event in ends:
-            ends[event]()
         elif kind == "P":
             event_p(which)
         elif kind == "Q":
@@ -276,7 +313,7 @@
         else:
             event_r(which)
 
-    wait("home", final.at[:, pl.ds(1, NZ - 1)])
+    wait("home", homes)
     for zz in range(NZ):
         for j in range(CHUNKS):
             for half in range(2):

time: 80.2 us -> 78.9 us (0.984)
  Pallas kernels: 78.2 us -> 76.9 us
    pallas_call x1, Pallas kernels: 78.2 us -> 76.9 us  [body(): pl.pallas_call(kernel, out_shape=jax.ShapeDtypeStruct((ROWS, NZ * PAIR),...]
where the time goes in v3:
time: 78.9 us; the launch traced here: 78.7 us
  Pallas kernels  76.9 us (97%)
  local copies, waits for them, and re-layouts  1.82 us (2%)
    pallas_call x1, Pallas kernels, body(): pl.pallas_call(kernel, out_shape=jax.ShapeDtypeStruct((ROWS, NZ * PAIR),...  76.9 us
    unnamed x1, local copies, waits for them, and re-layouts  1.82 us

profile of v3, /device:TPU:1, one launch (start us, length us, event | category | flops | bytes accessed | tf_op | source)
XLA Modules:
  0.0 78.7 jit_solution(12969870956594999254)
XLA Ops:
  0.0 76.9 %shard_map.28 = bf16[16,14336]{1,0:T(8,128)(2,1)} custom-call(bf16[16,14336]{1,0:T(8,128)(2,1)} %a_ref.1, bf16[896,896]{1,0:T(8,128)(2,1)} %b_ref.1), custom_call_target="tpu_custom_call" | custom-call | flops 6576668672 | bytes 4194304 | tf_op jit(solution)/shard_map/pallas_call | solution.py:326
  76.9 1.8 %copy.4 = bf16[16,14336]{1,0:T(8,128)(2,1)} copy(bf16[16,14336]{1,0:T(8,128)(2,1)} %shard_map.28) | data formatting | bytes 917504

commit v4 on v3

--- a/solution.py
+++ b/solution.py
@@ -22,6 +22,7 @@
 SLOTS = (0, 1, -1, 2, -2, 3, -3, 4)
 SLOT_OF = {d: s for s, d in enumerate(SLOTS)}
 SLOT_ROWS = NY * ROWS
+VMEM = 427 << 17
 SEMS = 83
 SENDS = {
     None: ((0, 0), (0, 1), (1, 0)),
@@ -339,7 +340,7 @@
             pltpu.VMEM((2, NY - 1, NZ, ROWS, LANES), F32),
             pltpu.SemaphoreType.DMA((SEMS,)),
         ],
-        compiler_params=pltpu.CompilerParams(collective_id=0, has_side_effects=True, vmem_limit_bytes=56 << 20),
+        compiler_params=pltpu.CompilerParams(collective_id=0, has_side_effects=True, vmem_limit_bytes=VMEM),
         cost_estimate=pl.CostEstimate(flops=2 * 512 * DEEP * PAIR, bytes_accessed=4 << 20, transcendentals=0),
     )(amplitudes, integrals)
 

time: 78.9 us -> 77 us (0.976)
  local copies, waits for them, and re-layouts: 1.82 us -> 0.77 us
  Pallas kernels: 76.9 us -> 76.1 us
    unnamed x1, local copies, waits for them, and re-layouts: 1.82 us -> 0.77 us
where the time goes in v4:
time: 77 us; the launch traced here: 76.9 us
  Pallas kernels  76.1 us (99%)
  local copies, waits for them, and re-layouts  0.77 us (1%)
    pallas_call x1, Pallas kernels, body(): pl.pallas_call(kernel, out_shape=jax.ShapeDtypeStruct((ROWS, NZ * PAIR),...  76.1 us

profile of v4, /device:TPU:1, one launch (start us, length us, event | category | flops | bytes accessed | tf_op | source)
XLA Modules:
  0.0 76.9 jit_solution(12854108852537077556)
XLA Ops:
  0.0 76.1 %shard_map.28 = bf16[16,14336]{1,0:T(8,128)(2,1)S(1)} custom-call(bf16[16,14336]{1,0:T(8,128)(2,1)} %a_ref.1, bf16[896,896]{1,0:T(8,128)(2,1)} %b_ref.1), custom_call_target="tpu_custom_call" | custom-call | flops 6576668672 | bytes 4194304 | tf_op jit(solution)/shard_map/pallas_call | solution.py:327
  76.2 0.8 %copy.4 = bf16[16,14336]{1,0:T(8,128)(2,1)} copy(bf16[16,14336]{1,0:T(8,128)(2,1)S(1)} %shard_map.28) | data formatting | bytes 917504

commit v5 on v4

--- a/solution.py
+++ b/solution.py
@@ -52,8 +52,8 @@
     "A21", "B12", "A23", "B13", "Pb", "B21", "Qa", "A22", "B30", "Pc", "A30", "B22", "Qb", "Ra", "A31", "B23",
     "Pd", "B31", "Qc", "A33", "B40", "Rb", "A32", "Pe", "B32", "Qd", "B33", "Pf", "B41", "A40", "Qe", "B50",
     "O4P", "Rc", "Pg", "B42", "Rd", "B43", "F4P", "B51", "Qf", "O4Q", "B52", "Qg", "O5P", "B60", "B53", "F5P",
-    "F4Q", "B61", "Re", "O5Q", "O6P", "B62", "O4R", "F5Q", "B63", "F6P", "Rf", "Rg", "F4R", "O5R", "O6R", "O6S",
-    "F5R", "F6R", "F6S",
+    "F4Q", "B61", "O6E", "Re", "O5Q", "O6P", "B62", "F6E", "O4R", "F5Q", "B63", "F6P", "Rf", "Rg", "F4R", "O5R",
+    "O6R", "O6S", "F5R", "F6R", "F6S",
 )
 
 
@@ -263,13 +263,26 @@
         wait(("near", j, own), second.at[j, 0])
         settle(j, pl.ds(0, NZ), here, part[j, :, y, :, here] + second[j, 0, :, :, here] + second[j, 1, :, :, here])
 
+    def block(near, dk):
+        xx = 1 - x % 2 if near else x % 2
+        return pl.ds(pl.multiple_of((xx * 2 + (core + dk) % 2) * BLOCK, LANES), BLOCK)
+
+    def last_e(own):
+        here = lane(own)
+        for ss in halves:
+            if own:
+                part[LAST, ss] = share(LAST, ss, block(True, 0), pl.ds(0, WIDE), WIDE)
+            part[LAST, ss, :, :, here] += share(LAST, ss, block(False, 0), here, LANES)
+
     def last_p(own):
         here = lane(own)
         if own:
-            own_products(LAST)
+            wait(("twin", LAST), ints.at[LAST, pl.ds(0, 3 * BLOCK), pl.ds(0, LANES)])
         for half in (1, 0):
             ss = halves[half]
-            part[LAST, ss, :, :, here] += share(LAST, ss, deep(False), here, LANES)
+            if own:
+                part[LAST, ss] += share(LAST, ss, block(True, 1), pl.ds(0, WIDE), WIDE)
+            part[LAST, ss, :, :, here] += share(LAST, ss, block(False, 1), here, LANES)
             for d in (2, 1, 3):
                 put("rest", ("rest", own, half), part.at[LAST, ss, (y + d) % NY, :, here], rest.at[int(own), d - 1, ss], at(dy=d))
 
@@ -291,6 +304,7 @@
 
     ends = {}
     for part_of, own in (("O", True), ("F", False)):
+        ends[f"{part_of}6E"] = functools.partial(last_e, own)
         ends[f"{part_of}6P"] = functools.partial(last_p, own)
         ends[f"{part_of}6R"] = functools.partial(last_r, own, 1)
         ends[f"{part_of}6S"] = functools.partial(last_r, own, 0)

time: 77 us -> 76.7 us (level)
  no operation moved by 1% of the time
where the time goes in v5:
time: 76.7 us
  Pallas kernels  75.9 us (99%)
  local copies, waits for them, and re-layouts  0.77 us (1%)
    pallas_call x1, Pallas kernels, body(): pl.pallas_call(kernel, out_shape=jax.ShapeDtypeStruct((ROWS, NZ * PAIR),...  75.9 us

profile of v5, /device:TPU:1, one launch (start us, length us, event | category | flops | bytes accessed | tf_op | source)
XLA Modules:
  0.0 76.7 jit_solution(13643018469788704954)
XLA Ops:
  0.0 75.9 %shard_map.28 = bf16[16,14336]{1,0:T(8,128)(2,1)S(1)} custom-call(bf16[16,14336]{1,0:T(8,128)(2,1)} %a_ref.1, bf16[896,896]{1,0:T(8,128)(2,1)} %b_ref.1), custom_call_target="tpu_custom_call" | custom-call | flops 6576668672 | bytes 4194304 | tf_op jit(solution)/shard_map/pallas_call | solution.py:341
  75.9 0.8 %copy.4 = bf16[16,14336]{1,0:T(8,128)(2,1)} copy(bf16[16,14336]{1,0:T(8,128)(2,1)S(1)} %shard_map.28) | data formatting | bytes 917504

commit v6 on v5

--- a/solution.py
+++ b/solution.py
@@ -51,7 +51,7 @@
     "S1", "S3", "B00", "S2", "A10", "B01", "A11", "B10", "A13", "B02", "A12", "B03", "Pa", "B11", "A20", "B20",
     "A21", "B12", "A23", "B13", "Pb", "B21", "Qa", "A22", "B30", "Pc", "A30", "B22", "Qb", "Ra", "A31", "B23",
     "Pd", "B31", "Qc", "A33", "B40", "Rb", "A32", "Pe", "B32", "Qd", "B33", "Pf", "B41", "A40", "Qe", "B50",
-    "O4P", "Rc", "Pg", "B42", "Rd", "B43", "F4P", "B51", "Qf", "O4Q", "B52", "Qg", "O5P", "B60", "B53", "F5P",
+    "O4P", "Rc", "B42", "Pg", "Rd", "B43", "F4P", "B51", "Qf", "O4Q", "B52", "O5P", "B60", "B53", "F5P", "Qg",
     "F4Q", "B61", "O6E", "Re", "O5Q", "O6P", "B62", "F6E", "O4R", "F5Q", "B63", "F6P", "Rf", "Rg", "F4R", "O5R",
     "O6R", "O6S", "F5R", "F6R", "F6S",
 )

time: 76.7 us -> 76.4 us (level)
  no operation moved by 1% of the time
where the time goes in v6:
time: 76.4 us
  Pallas kernels  75.6 us (99%)
  local copies, waits for them, and re-layouts  0.77 us (1%)
    pallas_call x1, Pallas kernels, body(): pl.pallas_call(kernel, out_shape=jax.ShapeDtypeStruct((ROWS, NZ * PAIR),...  75.6 us

profile of v6, /device:TPU:1, one launch (start us, length us, event | category | flops | bytes accessed | tf_op | source)
XLA Modules:
  0.0 76.4 jit_solution(2704425759075805524)
XLA Ops:
  0.0 75.6 %shard_map.28 = bf16[16,14336]{1,0:T(8,128)(2,1)S(1)} custom-call(bf16[16,14336]{1,0:T(8,128)(2,1)} %a_ref.1, bf16[896,896]{1,0:T(8,128)(2,1)} %b_ref.1), custom_call_target="tpu_custom_call" | custom-call | flops 6576668672 | bytes 4194304 | tf_op jit(solution)/shard_map/pallas_call | solution.py:341
  75.6 0.8 %copy.4 = bf16[16,14336]{1,0:T(8,128)(2,1)} copy(bf16[16,14336]{1,0:T(8,128)(2,1)S(1)} %shard_map.28) | data formatting | bytes 917504
